TPU v7x, 32 devices: a whole 2x2x4 slice. The times are simulated.
32 devices in a mesh: pipe: 4 (over y, core), dp: 4 (over z), tensor: 2 (over x).
Axes of the slice: x: 2, y: 2, z: 4, core: 2. Of those that a mesh axis runs over, the one named last changes fastest.
Arguments:
- activations: bfloat16 [4, 2, 512, 16384], P('pipe', None, 'dp', 'tensor'), may hold values from -6 to 6
- cotangent: bfloat16 [4, 2, 512, 1024], P('pipe', None, 'dp', 'tensor'), may hold values from -0.5 to 0.5
- error_tiles: bfloat16 [4, 4, 2, 2, 1, 128, 128], P('pipe', 'dp', 'tensor'), may hold values from -4 to 4
- tile_picks: int32 [4, 4, 2, 2, 1, 2], P('pipe', None, 'tensor'), may hold values from 0 to 63, as said below
- row_owners: int32 [4, 2, 64], P('pipe', 'tensor'), may hold values from 0 to 63, as said below
Outputs:
- grad_strips: bfloat16 [4, 2, 8192, 1024], P('pipe', 'tensor', 'dp')
Inputs may be any that keep to these rules, and one draw needn't show every extreme that they name: `tile_picks`: for each section, replica and row group, the 2 picked row blocks j have distinct owners row_owners[p, u, j] // 16; c is below 4. Each row_owners[p, u] is a permutation of 0 to 63.
All inputs are finite; a program needn't handle non-finite values.
Results may differ from a plain program's by a relative error of at most 0.001.
Values may be sent and summed in bfloat16 or wider, within the bound.
No kernel may reach another device: no remote copies, remote signals or barrier semaphores. Data moves between devices by JAX's collectives and lax.ppermute only.
A program may use at most 64 MiB of HBM per device.

v0:
```python
import functools

import jax
import jax.numpy as jnp
from jax import lax
from jax.experimental import pallas as pl
from jax.experimental.pallas import tpu as pltpu
from jax.sharding import PartitionSpec as P

VMEM = pl.BlockSpec(memory_space=pltpu.VMEM)
SMEM = pl.BlockSpec(memory_space=pltpu.SMEM)
ANY = pl.BlockSpec(memory_space=pl.ANY)
MOST_STEPS = 8
ROUNDS = {4: [(2, 3, 1, 0), (2, 0, 3, 1), (1, 3, 0, 2), (3, 2, 0, 1)]}
SMALL = pltpu.CompilerParams(vmem_limit_bytes=4 << 20)


def in_hbm(value):
    return pltpu.with_memory_space_constraint(value, pltpu.HBM)


def column(index, edge):
    return pl.ds(pl.multiple_of(index * edge, edge), edge)


def rounds(replicas):
    shifts = [
        tuple((one + step) % replicas for one in range(replicas)) for step in range(1, replicas)
    ]
    return ROUNDS.get(replicas, shifts)


def step_table(replicas):
    table = []
    for source in range(replicas):
        steps = [0] * replicas
        for step, targets in reversed(list(enumerate(rounds(replicas), 1))):
            steps[targets[source]] = step
        table.append(sum(step << 4 * target for target, step in enumerate(steps)))
    return table


def plan_sizes(tiles, steps):
    return 1, 1 + tiles, 1 + 2 * tiles, 1 + 2 * tiles + steps, 1 + 2 * tiles + 2 * steps


def pick(shifts, apart, columns, picks, owners, activations, errors, picked, plan, *refs):
    cuts, (read, seen, copied) = refs[:shifts], refs[shifts:]
    replica, group_at = lax.axis_index("dp"), lax.axis_index("tensor")
    groups, slots, replicas = picks.shape[2], picks.shape[3], picks.shape[-1]
    edge = picked.shape[1]
    tiles = [(group, slot) for group in range(groups) for slot in range(slots)]
    reads = []
    for at, (group, slot) in enumerate(tiles):
        block = picks[0, 0, group, slot, 0, replica]
        reads.append(
            pltpu.make_async_copy(
                activations.at[0, :, :, column(block, edge)], read.at[at], copied.at[at]
            )
        )
    for shift, cut in enumerate(cuts):
        other = lax.rem(group_at + groups - shift - 1, groups)
        reads.append(
            pltpu.make_async_copy(errors.at[0, 0, 0, other], cut, copied.at[len(tiles) + shift])
        )
    for copy in reads:
        copy.start()

    owned = owners.shape[-1] // replicas
    per_group = columns // groups
    steps = len(rounds(replicas)) + 1 if apart else replicas
    to_step, to_column, to_row, to_col, end = plan_sizes(len(tiles), steps)
    table = step_table(replicas) if apart else []
    mine = jnp.int32(0)
    for source, packed in enumerate(table):
        mine = jnp.where(replica == source, packed, mine)
    for at in range(to_row, end):
        plan[at] = -1

    for at, (group, slot) in enumerate(tiles):
        row = owners[0, 0, picks[0, 0, group, slot, 0, replica]]
        owner = jnp.int32(0)
        for one in range(1, replicas):
            owner += (row >= one * owned).astype(jnp.int32)
        plan[to_step + at] = (mine >> 4 * owner) & 15 if apart else owner
        plan[to_column + at] = picks[0, 0, group, slot, 1, replica]

    for origin in range(replicas):
        place_row, place_col = jnp.int32(-1), jnp.int32(0)
        for group, slot in tiles:
            row = owners[0, 0, picks[0, 0, group, slot, 0, origin]] - replica * owned
            here = (row >= 0) & (row < owned)
            place_row = jnp.where(here, row, place_row)
            place_col = jnp.where(
                here, picks[0, 0, group, slot, 1, origin] + group * per_group, place_col
            )
        step = (jnp.int32(table[origin]) >> 4 * replica) & 15 if apart else origin
        plan[to_row + step] = place_row
        plan[to_col + step] = place_col

    meets = jnp.int32(0)
    if apart:
        spots = [
            picks[0, 0, group, slot, 0, origin] * columns
            + picks[0, 0, group, slot, 1, origin]
            + group * per_group
            for group, slot in tiles
            for origin in range(replicas)
        ]
        for spot in spots:
            seen[spot] = 0
        for spot in spots:
            meets = meets | seen[spot]
            seen[spot] = 1
    plan[0] = meets

    for at, copy in enumerate(reads):
        copy.wait()
        if at < len(tiles):
            picked[at] = read[at].reshape(-1, edge).T


def clear(after, strip, zeros, cleared):
    zeros[...] = jnp.zeros_like(zeros)
    rows = zeros.shape[0]
    writes = [
        pltpu.make_async_copy(zeros, strip.at[0, 0, pl.ds(part * rows, rows)], cleared.at[part])
        for part in range(strip.shape[2] // rows)
    ]
    for write in writes:
        write.start()
    for write in writes:
        write.wait()


def multiply(groups, apart, to_step, to_column, plan, picked, error, *refs):
    returned, carried, outs = refs[:groups], refs[groups : 2 * groups - 1], refs[2 * groups - 1 :]
    mine = lax.axis_index("tensor")
    slots, (edge, tokens) = error.shape[4], picked.shape[1:]
    for shift in range(groups):
        group = lax.rem(mine + shift, groups)
        for slot in range(slots):
            at = group * slots + slot
            right = returned[shift][0, :, :, column(plan[to_column + at], edge)]
            extra = error[0, 0, 0, mine, slot] if shift == 0 else carried[shift - 1][slot]
            tile = jnp.dot(
                picked[at], right.reshape(tokens, edge), preferred_element_type=jnp.float32
            )
            tile = tile + extra.astype(jnp.float32)
            step = plan[to_step + at]
            if apart:
                outs[0][at] = tile
                store(tile.astype(jnp.bfloat16), step, outs[1:])
            else:
                outs[0][step] = tile


def store(tile, step, buffers):
    for at, buffer in enumerate(buffers):

        @pl.when(step == at)
        def _():
            buffer[...] = tile


def spread(to_step, plan, tiles, *buffers):
    for at in range(tiles.shape[0]):
        store(tiles[at], plan[to_step + at], buffers)


def place(count, alone, to_row, to_col, plan, *refs):
    blocks, strip, staged, sent = refs[:count], refs[-3], refs[-2], refs[-1]
    steps, edge = staged.shape[0], staged.shape[-1]

    def meets(one, other):
        return (plan[to_row + one] == plan[to_row + other]) & (
            plan[to_col + one] == plan[to_col + other]
        )

    def block_of(step):
        return blocks[0][step] if count == 1 else blocks[step][...]

    def first_of(step):
        first = plan[to_row + step] >= 0
        for earlier in range(0 if alone else step):
            first = first & jnp.logical_not(meets(earlier, step))
        return first

    def write_of(step):
        row, col = plan[to_row + step], plan[to_col + step]
        return pltpu.make_async_copy(
            blocks[step] if alone else staged.at[step],
            strip.at[0, 0, column(row, edge), column(col, edge)],
            sent.at[step],
        )

    for step in range(steps):

        @pl.when(first_of(step))
        def _():
            if not alone:
                total = block_of(step)
                for later in range(step + 1, steps):
                    total = total + jnp.where(meets(step, later), block_of(later), 0.0)
                staged[step] = total.astype(staged.dtype)
            write_of(step).start()

    for step in range(steps):

        @pl.when(first_of(step))
        def _():
            write_of(step).wait()


def body(mesh, activations, cotangent, error_tiles, tile_picks, row_owners):
    sections, replicas, groups = mesh.shape["pipe"], mesh.shape["dp"], mesh.shape["tensor"]
    edge = error_tiles.shape[-1]
    slots = tile_picks.shape[4]
    micro, tokens = activations.shape[1:3]
    width = cotangent.shape[-1] * groups
    strip_rows = row_owners.shape[-1] // replicas * edge
    picks = jnp.transpose(tile_picks, (0, 2, 3, 4, 5, 1))

    returned = []
    for shift in range(groups):
        pairs = [
            (
                (section + 1) % sections * groups + (group + shift) % groups,
                section * groups + group,
            )
            for section in range(sections)
            for group in range(groups)
        ]
        returned.append(lax.ppermute(cotangent, ("pipe", "tensor"), pairs))
    apart = replicas <= MOST_STEPS
    tiles, shifts = groups * slots, groups - 1
    steps = len(rounds(replicas)) + 1 if apart else replicas
    picked, plan, *errors = pl.pallas_call(
        functools.partial(pick, shifts, apart, width // edge),
        out_shape=[
            pltpu.VMEM((tiles, edge, micro * tokens), activations.dtype),
            jax.ShapeDtypeStruct((plan_sizes(tiles, steps)[-1],), jnp.int32),
        ]
        + [pltpu.VMEM((slots, edge, edge), error_tiles.dtype)] * shifts,
        in_specs=[SMEM, SMEM, ANY, ANY],
        out_specs=[VMEM, SMEM] + [VMEM] * shifts,
        scratch_shapes=[
            pltpu.VMEM((tiles, micro, tokens, edge), activations.dtype),
            pltpu.SMEM((row_owners.shape[-1] * (width // edge),), jnp.int32),
            pltpu.SemaphoreType.DMA((tiles + shifts,)),
        ],
        compiler_params=SMALL,
        name="pick",
    )(in_hbm(picks), in_hbm(row_owners), in_hbm(activations), in_hbm(error_tiles))
    carried = [
        lax.ppermute(
            error, "tensor", [((group + shift + 1) % groups, group) for group in range(groups)]
        )
        for shift, error in enumerate(errors)
    ]

    zero_rows = min(strip_rows, 256)
    strip_shape = (1, 1, strip_rows, width)
    cleared = pl.pallas_call(
        clear,
        out_shape=pltpu.HBM(strip_shape, jnp.bfloat16),
        in_specs=[ANY],
        out_specs=pl.BlockSpec(memory_space=pltpu.HBM),
        scratch_shapes=[
            pltpu.VMEM((zero_rows, width), jnp.bfloat16),
            pltpu.SemaphoreType.DMA((strip_rows // zero_rows,)),
        ],
        compiler_params=SMALL,
        cost_estimate=pl.CostEstimate(
            flops=0, bytes_accessed=2 * strip_rows * width, transcendentals=0
        ),
        name="clear",
    )(picked)

    to_step, to_column, to_row, to_col, _ = plan_sizes(tiles, steps)
    tile_shape = (edge, edge)
    if apart:
        out_shape = [jax.ShapeDtypeStruct((tiles,) + tile_shape, jnp.float32)]
        out_shape += [jax.ShapeDtypeStruct(tile_shape, jnp.bfloat16)] * steps
    else:
        out_shape = [jax.ShapeDtypeStruct((replicas,) + tile_shape, jnp.float32)]
    outgoing = pl.pallas_call(
        functools.partial(multiply, groups, apart, to_step, to_column),
        out_shape=out_shape,
        in_specs=[SMEM] + [VMEM] * (2 * groups + 1),
        out_specs=[VMEM] * len(out_shape),
        compiler_params=SMALL,
        name="multiply",
    )(plan, picked, error_tiles, *returned, *carried)

    def placed(alone, incoming):
        return pl.pallas_call(
            functools.partial(place, len(incoming), alone, to_row, to_col),
            out_shape=jax.ShapeDtypeStruct(strip_shape, jnp.bfloat16),
            in_specs=[SMEM] + [VMEM] * len(incoming) + [ANY],
            out_specs=ANY,
            scratch_shapes=[
                pltpu.VMEM((steps,) + tile_shape, jnp.bfloat16),
                pltpu.SemaphoreType.DMA((steps,)),
            ],
            input_output_aliases={1 + len(incoming): 0},
            compiler_params=SMALL,
            name="place",
        )(plan, *incoming, cleared)

    def exchanged(blocks):
        moved = [
            lax.ppermute(block, "dp", list(enumerate(targets)))
            for block, targets in zip(blocks[1:], rounds(replicas))
        ]
        return [blocks[0], *moved]

    def in_full():
        blocks = pl.pallas_call(
            functools.partial(spread, to_step),
            out_shape=[jax.ShapeDtypeStruct(tile_shape, jnp.float32)] * steps,
            in_specs=[SMEM, VMEM],
            out_specs=[VMEM] * steps,
            compiler_params=SMALL,
            name="spread",
        )(plan, outgoing[0])
        return placed(False, exchanged(blocks))

    if not apart:
        swapped = lax.all_to_all(outgoing[0], "dp", split_axis=0, concat_axis=0, tiled=True)
        return placed(False, [swapped])
    return lax.cond(plan[0] > 0, in_full, lambda: placed(True, exchanged(outgoing[1:])))


def solution(mesh):
    in_specs = (
        P("pipe", None, "dp", "tensor"),
        P("pipe", None, "dp", "tensor"),
        P("pipe", "dp", "tensor", None, None, None, None),
        P("pipe", None, "tensor", None, None, None),
        P("pipe", "tensor", None),
    )
    out_specs = P("pipe", "tensor", "dp", None)
    return jax.shard_map(
        functools.partial(body, mesh),
        mesh=mesh,
        in_specs=in_specs,
        out_specs=out_specs,
        check_vma=False,
    )
```

profile of v0, /device:TPU:0, one launch (start us, length us, event | category | flops | bytes accessed | tf_op | source)
XLA Modules:
  0.0 22.6 jit_solution(5910980095714668079)
XLA Ops:
  0.0 3.3 %collective-permute-start.9 = (bf16[1,2,128,512]{3,2,1,0:T(8,128)(2,1)}, bf16[1,2,128,512]{3,2,1,0:T(8,128)(2,1)S(1)}, u32[]{:S(2)}, u32[]{:S(2)}) collective-permute-start(bf16[1,2,128,512]{3,2,1,0:T(8,128)(2,1)} %param.8), channel_id=1, source_target_pairs={{9,0},{8,1},{17,8},{16,9},{25,16},{24,17},{1,24},{0,25},{11,2},{10... | collective-permute-start | bytes 786440 | tf_op jit(solution)/shard_map/ppermute | solution.py:234
  3.3 0.8 %collective-permute-start.8 = (bf16[1,2,128,512]{3,2,1,0:T(8,128)(2,1)}, bf16[1,2,128,512]{3,2,1,0:T(8,128)(2,1)S(1)}, u32[]{:S(2)}, u32[]{:S(2)}) collective-permute-start(bf16[1,2,128,512]{3,2,1,0:T(8,128)(2,1)} %param.8), channel_id=1, source_target_pairs={{8,0},{9,1},{16,8},{17,9},{24,16},{25,17},{0,24},{1,25},{10,2},{11... | collective-permute-start | bytes 786440 | tf_op jit(solution)/shard_map/ppermute | solution.py:234
  4.2 0.0 copy-start
  4.2 2.4 %pick.1 = (bf16[2,128,256]{2,1,0:T(8,128)(2,1)S(1)}, s32[15]{0:T(128)S(1)}, bf16[1,128,128]{2,1,0:T(8,128)(2,1)S(1)}) custom-call(s32[1,1,2,1,2,4]{5,4,3,2,1,0:T(2,128)} %bitcast.4, s32[1,1,64]{2,1,0:T(1,128)} %owners.1, bf16[1,2,128,8192]{3,2,1,0:T(8,128)(2,1)} %activations.1, bf16[1,1,1,2,1,128,128]{6,5,4,3,2,1,0:T(8,128)(2,1)} %error.1), custom_call_target="tpu_custom_call" | custom-call | tf_op jit(solution)/shard_map/pick/pallas_call | solution.py:238
  6.6 0.6 %collective-permute-start.10 = (bf16[1,128,128]{2,1,0:T(8,128)(2,1)S(1)}, bf16[1,128,128]{2,1,0:T(8,128)(2,1)S(1)}, u32[]{:S(2)}, u32[]{:S(2)}) collective-permute-start(bf16[1,128,128]{2,1,0:T(8,128)(2,1)S(1)} %get-tuple-element.54), channel_id=1, source_target_pairs={{1,0},{0,1},{3,2},{2,3},{5,4},{4,5},{7,6},{6,7},{9,8},{8,9},{11,10... | collective-permute-start | bytes 98312 | tf_op jit(solution)/shard_map/ppermute | solution.py:256
  7.3 2.1 %clear.1 = bf16[1,1,2048,1024]{3,2,1,0:T(8,128)(2,1)} custom-call(bf16[2,128,256]{2,1,0:T(8,128)(2,1)S(1)} %get-tuple-element.53.picked.after), custom_call_target="tpu_custom_call" | custom-call | bytes 4194304 | tf_op jit(solution)/shard_map/clear/pallas_call | solution.py:264
  9.4 1.2 %collective-permute-done.10.refs_2_ = bf16[1,128,128]{2,1,0:T(8,128)(2,1)S(1)} collective-permute-done((bf16[1,128,128]{2,1,0:T(8,128)(2,1)S(1)}, bf16[1,128,128]{2,1,0:T(8,128)(2,1)S(1)}, u32[]{:S(2)}, u32[]{:S(2)}) %collective-permute-start.10) | collective-permute-done | bytes 32800 | tf_op jit(solution)/shard_map/ppermute | solution.py:256
  10.6 0.0 collective-permute-done.9.refs_1_
  10.6 0.2 collective-permute-done.8.refs_0_
  10.8 0.0 copy-done
  10.8 0.9 %multiply.1 = (f32[2,128,128]{2,1,0:T(8,128)S(1)}, bf16[128,128]{1,0:T(8,128)(2,1)S(1)}, bf16[128,128]{1,0:T(8,128)(2,1)S(1)}, bf16[128,128]{1,0:T(8,128)(2,1)S(...) custom-call(s32[15]{0:T(128)S(1)} %get-tuple-element.52.plan, ...), custom_call_target="tpu_custom_call" | custom-call | tf_op jit(solution)/shard_map/multiply/pallas_call | solution.py:287
  11.7 10.9 %conditional.1 = (bf16[1,1,2048,1024]{3,2,1,0:T(8,128)(2,1)}) conditional(s32[]{:T(128)} %bitcast.1, (bf16[128,128]{1,0:T(8,128)(2,1)S(1)}, bf16[128,128]{1,0:T(8,128)(2,1)S(1)}, bf16[128,128]{1,0:T(8,128)(2,1)S(1)}, bf16[128,128]{1,0:T(8,128)(2,1)S(1)}, s32[15]{0:T(128)S(1)}, /*index=5*/bf16[128,128]{1,0:T(8,128)(2,1)S(1)}, ...), branch_computations={%region_0.0_spmd, %region_1.0_spmd} | conditional | bytes 1048744 | solution.py:332
  11.7 2.8 %collective-permute-start = (bf16[128,128]{1,0:T(8,128)(2,1)S(1)}, bf16[128,128]{1,0:T(8,128)(2,1)S(1)}, u32[]{:S(2)}, u32[]{:S(2)}) collective-permute-start(bf16[128,128]{1,0:T(8,128)(2,1)S(1)} %get-tuple-element.30), channel_id=1, source_target_pairs={{0,4},{2,6},{4,2},{6,0},{1,5},{3,7},{5,3},{7,1},{8,12},{10,14},{12... | collective-permute-start | bytes 98312 | tf_op jit(solution)/shard_map/cond/branch_0_fun/ppermute | solution.py:313
  14.6 0.5 %collective-permute-start.1 = (bf16[128,128]{1,0:T(8,128)(2,1)S(1)}, bf16[128,128]{1,0:T(8,128)(2,1)S(1)}, u32[]{:S(2)}, u32[]{:S(2)}) collective-permute-start(bf16[128,128]{1,0:T(8,128)(2,1)S(1)} %get-tuple-element.31), channel_id=1, source_target_pairs={{0,4},{2,0},{4,6},{6,2},{1,5},{3,1},{5,7},{7,3},{8,12},{10,8},{12,... | collective-permute-start | bytes 98312 | tf_op jit(solution)/shard_map/cond/branch_0_fun/ppermute | solution.py:313
  15.0 1.6 %collective-permute-start.2 = (bf16[128,128]{1,0:T(8,128)(2,1)S(1)}, bf16[128,128]{1,0:T(8,128)(2,1)S(1)}, u32[]{:S(2)}, u32[]{:S(2)}) collective-permute-start(bf16[128,128]{1,0:T(8,128)(2,1)S(1)} %get-tuple-element.32), channel_id=1, source_target_pairs={{0,2},{2,6},{4,0},{6,4},{1,3},{3,7},{5,1},{7,5},{8,10},{10,14},{12... | collective-permute-start | bytes 98312 | tf_op jit(solution)/shard_map/cond/branch_0_fun/ppermute | solution.py:313
  16.6 1.9 %collective-permute-start.3 = (bf16[128,128]{1,0:T(8,128)(2,1)S(1)}, bf16[128,128]{1,0:T(8,128)(2,1)S(1)}, u32[]{:S(2)}, u32[]{:S(2)}) collective-permute-start(bf16[128,128]{1,0:T(8,128)(2,1)S(1)} %get-tuple-element.33), channel_id=1, source_target_pairs={{0,6},{2,4},{4,0},{6,2},{1,7},{3,5},{5,1},{7,3},{8,14},{10,12},{12... | collective-permute-start | bytes 98312 | tf_op jit(solution)/shard_map/cond/branch_0_fun/ppermute | solution.py:313
  18.5 0.0 collective-permute-done.refs_1_
  18.5 0.0 collective-permute-done.1.refs_2_
  18.5 2.1 %collective-permute-done.2.refs_3_ = bf16[128,128]{1,0:T(8,128)(2,1)S(1)} collective-permute-done((bf16[128,128]{1,0:T(8,128)(2,1)S(1)}, bf16[128,128]{1,0:T(8,128)(2,1)S(1)}, u32[]{:S(2)}, u32[]{:S(2)}) %collective-permute-start.2) | collective-permute-done | bytes 32800 | tf_op jit(solution)/shard_map/cond/branch_0_fun/ppermute | solution.py:313
  20.6 0.8 %collective-permute-done.3.refs_4_ = bf16[128,128]{1,0:T(8,128)(2,1)S(1)} collective-permute-done((bf16[128,128]{1,0:T(8,128)(2,1)S(1)}, bf16[128,128]{1,0:T(8,128)(2,1)S(1)}, u32[]{:S(2)}, u32[]{:S(2)}) %collective-permute-start.3) | collective-permute-done | bytes 32800 | tf_op jit(solution)/shard_map/cond/branch_0_fun/ppermute | solution.py:313
  21.4 1.2 %place.2 = bf16[1,1,2048,1024]{3,2,1,0:T(8,128)(2,1)} custom-call(s32[15]{0:T(128)S(1)} %get-tuple-element.28.plan, bf16[128,128]{1,0:T(8,128)(2,1)S(1)} %get-tuple-element.29.refs_0_, bf16[128,128]{1,0:T(8,128)(2,1)S(1)} %collective-permute-done.refs_1_, bf16[128,128]{1,0:T(8,128)(2,1)S(1)} %collective-permute-done.1.refs_2_, ...), custom_call_target="tpu_custom_call", output_to_operand_aliasing={{}: (6, {})} | custom-call | tf_op jit(solution)/shard_map/cond/branch_0_fun/place/pallas_call | solution.py:297
Async XLA Ops:
  0.0 10.6 %collective-permute-start.9 = (bf16[1,2,128,512]{3,2,1,0:T(8,128)(2,1)}, bf16[1,2,128,512]{3,2,1,0:T(8,128)(2,1)S(1)}, u32[]{:S(2)}, u32[]{:S(2)}) collective-permute-start(bf16[1,2,128,512]{3,2,1,0:T(8,128)(2,1)} %param.8), channel_id=1, source_target_pairs={{9,0},{8,1},{17,8},{16,9},{25,16},{24,17},{1,24},{0,25},{11,2},{10... | collective-permute-start | bytes 786440 | tf_op jit(solution)/shard_map/ppermute | solution.py:234
  3.3 7.5 %collective-permute-start.8 = (bf16[1,2,128,512]{3,2,1,0:T(8,128)(2,1)}, bf16[1,2,128,512]{3,2,1,0:T(8,128)(2,1)S(1)}, u32[]{:S(2)}, u32[]{:S(2)}) collective-permute-start(bf16[1,2,128,512]{3,2,1,0:T(8,128)(2,1)} %param.8), channel_id=1, source_target_pairs={{8,0},{9,1},{16,8},{17,9},{24,16},{25,17},{0,24},{1,25},{10,2},{11... | collective-permute-start | bytes 786440 | tf_op jit(solution)/shard_map/ppermute | solution.py:234
  4.2 6.6 %copy-start = (bf16[1,1,1,2,1,128,128]{6,5,4,3,2,1,0:T(8,128)(2,1)S(1)}, bf16[1,1,1,2,1,128,128]{6,5,4,3,2,1,0:T(8,128)(2,1)}, u32[]{:S(2)}) copy-start(bf16[1,1,1,2,1,128,128]{6,5,4,3,2,1,0:T(8,128)(2,1)} %error.1) | copy-start | bytes 196612
  6.6 4.0 %collective-permute-start.10 = (bf16[1,128,128]{2,1,0:T(8,128)(2,1)S(1)}, bf16[1,128,128]{2,1,0:T(8,128)(2,1)S(1)}, u32[]{:S(2)}, u32[]{:S(2)}) collective-permute-start(bf16[1,128,128]{2,1,0:T(8,128)(2,1)S(1)} %get-tuple-element.54), channel_id=1, source_target_pairs={{1,0},{0,1},{3,2},{2,3},{5,4},{4,5},{7,6},{6,7},{9,8},{8,9},{11,10... | collective-permute-start | bytes 98312 | tf_op jit(solution)/shard_map/ppermute | solution.py:256
  11.7 6.8 %collective-permute-start = (bf16[128,128]{1,0:T(8,128)(2,1)S(1)}, bf16[128,128]{1,0:T(8,128)(2,1)S(1)}, u32[]{:S(2)}, u32[]{:S(2)}) collective-permute-start(bf16[128,128]{1,0:T(8,128)(2,1)S(1)} %get-tuple-element.30), channel_id=1, source_target_pairs={{0,4},{2,6},{4,2},{6,0},{1,5},{3,7},{5,3},{7,1},{8,12},{10,14},{12... | collective-permute-start | bytes 98312 | tf_op jit(solution)/shard_map/cond/branch_0_fun/ppermute | solution.py:313
  14.6 3.9 %collective-permute-start.1 = (bf16[128,128]{1,0:T(8,128)(2,1)S(1)}, bf16[128,128]{1,0:T(8,128)(2,1)S(1)}, u32[]{:S(2)}, u32[]{:S(2)}) collective-permute-start(bf16[128,128]{1,0:T(8,128)(2,1)S(1)} %get-tuple-element.31), channel_id=1, source_target_pairs={{0,4},{2,0},{4,6},{6,2},{1,5},{3,1},{5,7},{7,3},{8,12},{10,8},{12,... | collective-permute-start | bytes 98312 | tf_op jit(solution)/shard_map/cond/branch_0_fun/ppermute | solution.py:313
  15.0 5.6 %collective-permute-start.2 = (bf16[128,128]{1,0:T(8,128)(2,1)S(1)}, bf16[128,128]{1,0:T(8,128)(2,1)S(1)}, u32[]{:S(2)}, u32[]{:S(2)}) collective-permute-start(bf16[128,128]{1,0:T(8,128)(2,1)S(1)} %get-tuple-element.32), channel_id=1, source_target_pairs={{0,2},{2,6},{4,0},{6,4},{1,3},{3,7},{5,1},{7,5},{8,10},{10,14},{12... | collective-permute-start | bytes 98312 | tf_op jit(solution)/shard_map/cond/branch_0_fun/ppermute | solution.py:313
  16.6 4.8 %collective-permute-start.3 = (bf16[128,128]{1,0:T(8,128)(2,1)S(1)}, bf16[128,128]{1,0:T(8,128)(2,1)S(1)}, u32[]{:S(2)}, u32[]{:S(2)}) collective-permute-start(bf16[128,128]{1,0:T(8,128)(2,1)S(1)} %get-tuple-element.33), channel_id=1, source_target_pairs={{0,6},{2,4},{4,0},{6,2},{1,7},{3,5},{5,1},{7,3},{8,14},{10,12},{12... | collective-permute-start | bytes 98312 | tf_op jit(solution)/shard_map/cond/branch_0_fun/ppermute | solution.py:313
where the time goes:
time: 22.8 us; the launch traced here: 22.6 us
  starting transfers between devices  11.5 us (50%)
  Pallas kernels  6.68 us (29%)
  waiting for transfers between devices  4.3 us (19%)
    ppermute x4, starting transfers between devices, exchanged(): lax.ppermute(block, 'dp', list(enumerate(targets)))  6.77 us
    ppermute x2, starting transfers between devices, body(): returned.append(lax.ppermute(cotangent, ('pipe', 'tensor'), pairs))  4.18 us
    ppermute x4, waiting for transfers between devices, exchanged(): lax.ppermute(block, 'dp', list(enumerate(targets)))  2.9 us
    pallas_call x1, Pallas kernels, body(): pl.pallas_call(functools.partial(pick, shifts, apart, width // edge), out...  2.44 us
    pallas_call x1, Pallas kernels, body(): pl.pallas_call(clear, out_shape=pltpu.HBM(strip_shape, jnp.bfloat16), in_...  2.1 us
    ppermute x1, waiting for transfers between devices, body(): lax.ppermute(error, 'tensor', [((group + shift + 1) % groups, group) for...  1.22 us
    pallas_call x1, Pallas kernels, placed(): pl.pallas_call(functools.partial(place, len(incoming), alone, to_row, to_...  1.21 us
    pallas_call x1, Pallas kernels, body(): pl.pallas_call(functools.partial(multiply, groups, apart, to_step, to_col...  0.92 us
  transfers between devices with their start and end apart: 7, of which 4 were waited for; matrix products, arithmetic and copies ran while one was open for 0% of the time, Pallas kernels for 20%

commit v1 on v0

--- a/solution.py
+++ b/solution.py
@@ -11,7 +11,7 @@
 SMEM = pl.BlockSpec(memory_space=pltpu.SMEM)
 ANY = pl.BlockSpec(memory_space=pl.ANY)
 MOST_STEPS = 8
-ROUNDS = {4: [(2, 3, 1, 0), (2, 0, 3, 1), (1, 3, 0, 2), (3, 2, 0, 1)]}
+ROUNDS = {4: [(2, 3, 1, 0), (3, 2, 0, 1), (1, 0, 3, 2)]}
 SMALL = pltpu.CompilerParams(vmem_limit_bytes=4 << 20)
 
 

time: 22.8 us -> 21.1 us (0.925)
  starting transfers between devices: 11.5 us -> 9.19 us
  waiting for transfers between devices: 4.3 us -> 4.99 us
    ppermute x4 -> x3, starting transfers between devices: 6.77 us -> 4.41 us  [exchanged(): lax.ppermute(block, 'dp', list(enumerate(targets)))]
    ppermute x4 -> x3, waiting for transfers between devices: 2.9 us -> 3.58 us  [exchanged(): lax.ppermute(block, 'dp', list(enumerate(targets)))]
  transfers between devices with their start and end apart: 7 -> 6, of which waited for: 4 -> 5; matrix products, arithmetic and copies ran while one was open for 0% -> 0% of each run, Pallas kernels for 20% -> 22%
where the time goes in v1:
time: 21.1 us; the launch traced here: 20.9 us
  starting transfers between devices  9.19 us (44%)
  Pallas kernels  6.66 us (32%)
  waiting for transfers between devices  4.99 us (24%)
    ppermute x3, starting transfers between devices, exchanged(): lax.ppermute(block, 'dp', list(enumerate(targets)))  4.41 us
    ppermute x2, starting transfers between devices, body(): returned.append(lax.ppermute(cotangent, ('pipe', 'tensor'), pairs))  4.18 us
    ppermute x3, waiting for transfers between devices, exchanged(): lax.ppermute(block, 'dp', list(enumerate(targets)))  3.58 us
    pallas_call x1, Pallas kernels, body(): pl.pallas_call(functools.partial(pick, shifts, apart, width // edge), out...  2.44 us
    pallas_call x1, Pallas kernels, body(): pl.pallas_call(clear, out_shape=pltpu.HBM(strip_shape, jnp.bfloat16), in_...  2.1 us
    ppermute x1, waiting for transfers between devices, body(): lax.ppermute(error, 'tensor', [((group + shift + 1) % groups, group) for...  1.22 us
    pallas_call x1, Pallas kernels, placed(): pl.pallas_call(functools.partial(place, len(incoming), alone, to_row, to_...  1.2 us
    pallas_call x1, Pallas kernels, body(): pl.pallas_call(functools.partial(multiply, groups, apart, to_step, to_col...  0.91 us
  transfers between devices with their start and end apart: 6, of which 5 were waited for; matrix products, arithmetic and copies ran while one was open for 0% of the time, Pallas kernels for 22%

profile of v1, /device:TPU:0, one launch (start us, length us, event | category | flops | bytes accessed | tf_op | source)
XLA Modules:
  0.0 20.9 jit_solution(16491815416906949253)
XLA Ops:
  0.0 3.3 %collective-permute-start.7 = (bf16[1,2,128,512]{3,2,1,0:T(8,128)(2,1)}, bf16[1,2,128,512]{3,2,1,0:T(8,128)(2,1)S(1)}, u32[]{:S(2)}, u32[]{:S(2)}) collective-permute-start(bf16[1,2,128,512]{3,2,1,0:T(8,128)(2,1)} %param.8), channel_id=1, source_target_pairs={{9,0},{8,1},{17,8},{16,9},{25,16},{24,17},{1,24},{0,25},{11,2},{10... | collective-permute-start | bytes 786440 | tf_op jit(solution)/shard_map/ppermute | solution.py:234
  3.3 0.8 %collective-permute-start.6 = (bf16[1,2,128,512]{3,2,1,0:T(8,128)(2,1)}, bf16[1,2,128,512]{3,2,1,0:T(8,128)(2,1)S(1)}, u32[]{:S(2)}, u32[]{:S(2)}) collective-permute-start(bf16[1,2,128,512]{3,2,1,0:T(8,128)(2,1)} %param.8), channel_id=1, source_target_pairs={{8,0},{9,1},{16,8},{17,9},{24,16},{25,17},{0,24},{1,25},{10,2},{11... | collective-permute-start | bytes 786440 | tf_op jit(solution)/shard_map/ppermute | solution.py:234
  4.2 0.0 copy-start
  4.2 2.4 %pick.1 = (bf16[2,128,256]{2,1,0:T(8,128)(2,1)S(1)}, s32[13]{0:T(128)S(1)}, bf16[1,128,128]{2,1,0:T(8,128)(2,1)S(1)}) custom-call(s32[1,1,2,1,2,4]{5,4,3,2,1,0:T(2,128)} %bitcast.4, s32[1,1,64]{2,1,0:T(1,128)} %owners.1, bf16[1,2,128,8192]{3,2,1,0:T(8,128)(2,1)} %activations.1, bf16[1,1,1,2,1,128,128]{6,5,4,3,2,1,0:T(8,128)(2,1)} %error.1), custom_call_target="tpu_custom_call" | custom-call | tf_op jit(solution)/shard_map/pick/pallas_call | solution.py:238
  6.6 0.6 %collective-permute-start.8 = (bf16[1,128,128]{2,1,0:T(8,128)(2,1)S(1)}, bf16[1,128,128]{2,1,0:T(8,128)(2,1)S(1)}, u32[]{:S(2)}, u32[]{:S(2)}) collective-permute-start(bf16[1,128,128]{2,1,0:T(8,128)(2,1)S(1)} %get-tuple-element.49), channel_id=1, source_target_pairs={{1,0},{0,1},{3,2},{2,3},{5,4},{4,5},{7,6},{6,7},{9,8},{8,9},{11,10... | collective-permute-start | bytes 98312 | tf_op jit(solution)/shard_map/ppermute | solution.py:256
  7.3 2.1 %clear.1 = bf16[1,1,2048,1024]{3,2,1,0:T(8,128)(2,1)} custom-call(bf16[2,128,256]{2,1,0:T(8,128)(2,1)S(1)} %get-tuple-element.48.picked.after), custom_call_target="tpu_custom_call" | custom-call | bytes 4194304 | tf_op jit(solution)/shard_map/clear/pallas_call | solution.py:264
  9.4 1.2 %collective-permute-done.8.refs_2_ = bf16[1,128,128]{2,1,0:T(8,128)(2,1)S(1)} collective-permute-done((bf16[1,128,128]{2,1,0:T(8,128)(2,1)S(1)}, bf16[1,128,128]{2,1,0:T(8,128)(2,1)S(1)}, u32[]{:S(2)}, u32[]{:S(2)}) %collective-permute-start.8) | collective-permute-done | bytes 32800 | tf_op jit(solution)/shard_map/ppermute | solution.py:256
  10.6 0.0 collective-permute-done.7.refs_1_
  10.6 0.2 collective-permute-done.6.refs_0_
  10.8 0.0 copy-done
  10.8 0.9 %multiply.1 = (f32[2,128,128]{2,1,0:T(8,128)S(1)}, bf16[128,128]{1,0:T(8,128)(2,1)S(1)}, bf16[128,128]{1,0:T(8,128)(2,1)S(1)}, bf16[128,128]{1,0:T(8,128)(2,1)S(1)}, bf16[128,128]{1,0:T(8,128)(2,1)S(1)}) custom-call(s32[13]{0:T(128)S(1)} %get-tuple-element.47.plan, bf16[2,128,256]{2,1,0:T(8,128)(2,1)S(1)} %get-tuple-element.48.picked.after, ...), custom_call_target="tpu_custom_call" | custom-call | tf_op jit(solution)/shard_map/multiply/pallas_call | solution.py:287
  11.7 9.2 %conditional.1 = (bf16[1,1,2048,1024]{3,2,1,0:T(8,128)(2,1)}) conditional(s32[]{:T(128)} %bitcast.1, (bf16[128,128]{1,0:T(8,128)(2,1)S(1)}, bf16[128,128]{1,0:T(8,128)(2,1)S(1)}, bf16[128,128]{1,0:T(8,128)(2,1)S(1)}, s32[13]{0:T(128)S(1)}, bf16[128,128]{1,0:T(8,128)(2,1)S(1)}, /*index=5*/bf16[1,1,2048,1024]{3,2,1,0:T(8,128)(2,1)}) %tuple.11, ...), branch_computations={%region_0.0_spmd, %region_1.0_spmd} | conditional | bytes 786560 | solution.py:332
  11.7 2.8 %collective-permute-start = (bf16[128,128]{1,0:T(8,128)(2,1)S(1)}, bf16[128,128]{1,0:T(8,128)(2,1)S(1)}, u32[]{:S(2)}, u32[]{:S(2)}) collective-permute-start(bf16[128,128]{1,0:T(8,128)(2,1)S(1)} %get-tuple-element.28), channel_id=1, source_target_pairs={{0,4},{2,6},{4,2},{6,0},{1,5},{3,7},{5,3},{7,1},{8,12},{10,14},{12... | collective-permute-start | bytes 98312 | tf_op jit(solution)/shard_map/cond/branch_0_fun/ppermute | solution.py:313
  14.6 1.1 %collective-permute-start.1 = (bf16[128,128]{1,0:T(8,128)(2,1)S(1)}, bf16[128,128]{1,0:T(8,128)(2,1)S(1)}, u32[]{:S(2)}, u32[]{:S(2)}) collective-permute-start(bf16[128,128]{1,0:T(8,128)(2,1)S(1)} %get-tuple-element.29), channel_id=1, source_target_pairs={{0,6},{2,4},{4,0},{6,2},{1,7},{3,5},{5,1},{7,3},{8,14},{10,12},{12... | collective-permute-start | bytes 98312 | tf_op jit(solution)/shard_map/cond/branch_0_fun/ppermute | solution.py:313
  15.6 0.5 %collective-permute-start.2 = (bf16[128,128]{1,0:T(8,128)(2,1)S(1)}, bf16[128,128]{1,0:T(8,128)(2,1)S(1)}, u32[]{:S(2)}, u32[]{:S(2)}) collective-permute-start(bf16[128,128]{1,0:T(8,128)(2,1)S(1)} %get-tuple-element.30), channel_id=1, source_target_pairs={{0,2},{2,0},{4,6},{6,4},{1,3},{3,1},{5,7},{7,5},{8,10},{10,8},{12,... | collective-permute-start | bytes 98312 | tf_op jit(solution)/shard_map/cond/branch_0_fun/ppermute | solution.py:313
  16.1 1.5 %collective-permute-done.refs_1_ = bf16[128,128]{1,0:T(8,128)(2,1)S(1)} collective-permute-done((bf16[128,128]{1,0:T(8,128)(2,1)S(1)}, bf16[128,128]{1,0:T(8,128)(2,1)S(1)}, u32[]{:S(2)}, u32[]{:S(2)}) %collective-permute-start) | collective-permute-done | bytes 32800 | tf_op jit(solution)/shard_map/cond/branch_0_fun/ppermute | solution.py:313
  17.6 1.8 %collective-permute-done.1.refs_2_ = bf16[128,128]{1,0:T(8,128)(2,1)S(1)} collective-permute-done((bf16[128,128]{1,0:T(8,128)(2,1)S(1)}, bf16[128,128]{1,0:T(8,128)(2,1)S(1)}, u32[]{:S(2)}, u32[]{:S(2)}) %collective-permute-start.1) | collective-permute-done | bytes 32800 | tf_op jit(solution)/shard_map/cond/branch_0_fun/ppermute | solution.py:313
  19.4 0.3 %collective-permute-done.2.refs_3_ = bf16[128,128]{1,0:T(8,128)(2,1)S(1)} collective-permute-done((bf16[128,128]{1,0:T(8,128)(2,1)S(1)}, bf16[128,128]{1,0:T(8,128)(2,1)S(1)}, u32[]{:S(2)}, u32[]{:S(2)}) %collective-permute-start.2) | collective-permute-done | bytes 32800 | tf_op jit(solution)/shard_map/cond/branch_0_fun/ppermute | solution.py:313
  19.7 1.2 %place.2 = bf16[1,1,2048,1024]{3,2,1,0:T(8,128)(2,1)} custom-call(s32[13]{0:T(128)S(1)} %get-tuple-element.26.plan, bf16[128,128]{1,0:T(8,128)(2,1)S(1)} %get-tuple-element.27.refs_0_, bf16[128,128]{1,0:T(8,128)(2,1)S(1)} %collective-permute-done.refs_1_, bf16[128,128]{1,0:T(8,128)(2,1)S(1)} %collective-permute-done.1.refs_2_, ...), custom_call_target="tpu_custom_call", output_to_operand_aliasing={{}: (5, {})} | custom-call | tf_op jit(solution)/shard_map/cond/branch_0_fun/place/pallas_call | solution.py:297
Async XLA Ops:
  0.0 10.6 %collective-permute-start.7 = (bf16[1,2,128,512]{3,2,1,0:T(8,128)(2,1)}, bf16[1,2,128,512]{3,2,1,0:T(8,128)(2,1)S(1)}, u32[]{:S(2)}, u32[]{:S(2)}) collective-permute-start(bf16[1,2,128,512]{3,2,1,0:T(8,128)(2,1)} %param.8), channel_id=1, source_target_pairs={{9,0},{8,1},{17,8},{16,9},{25,16},{24,17},{1,24},{0,25},{11,2},{10... | collective-permute-start | bytes 786440 | tf_op jit(solution)/shard_map/ppermute | solution.py:234
  3.3 7.5 %collective-permute-start.6 = (bf16[1,2,128,512]{3,2,1,0:T(8,128)(2,1)}, bf16[1,2,128,512]{3,2,1,0:T(8,128)(2,1)S(1)}, u32[]{:S(2)}, u32[]{:S(2)}) collective-permute-start(bf16[1,2,128,512]{3,2,1,0:T(8,128)(2,1)} %param.8), channel_id=1, source_target_pairs={{8,0},{9,1},{16,8},{17,9},{24,16},{25,17},{0,24},{1,25},{10,2},{11... | collective-permute-start | bytes 786440 | tf_op jit(solution)/shard_map/ppermute | solution.py:234
  4.2 6.6 %copy-start = (bf16[1,1,1,2,1,128,128]{6,5,4,3,2,1,0:T(8,128)(2,1)S(1)}, bf16[1,1,1,2,1,128,128]{6,5,4,3,2,1,0:T(8,128)(2,1)}, u32[]{:S(2)}) copy-start(bf16[1,1,1,2,1,128,128]{6,5,4,3,2,1,0:T(8,128)(2,1)} %error.1) | copy-start | bytes 196612
  6.6 4.0 %collective-permute-start.8 = (bf16[1,128,128]{2,1,0:T(8,128)(2,1)S(1)}, bf16[1,128,128]{2,1,0:T(8,128)(2,1)S(1)}, u32[]{:S(2)}, u32[]{:S(2)}) collective-permute-start(bf16[1,128,128]{2,1,0:T(8,128)(2,1)S(1)} %get-tuple-element.49), channel_id=1, source_target_pairs={{1,0},{0,1},{3,2},{2,3},{5,4},{4,5},{7,6},{6,7},{9,8},{8,9},{11,10... | collective-permute-start | bytes 98312 | tf_op jit(solution)/shard_map/ppermute | solution.py:256
  11.7 5.9 %collective-permute-start = (bf16[128,128]{1,0:T(8,128)(2,1)S(1)}, bf16[128,128]{1,0:T(8,128)(2,1)S(1)}, u32[]{:S(2)}, u32[]{:S(2)}) collective-permute-start(bf16[128,128]{1,0:T(8,128)(2,1)S(1)} %get-tuple-element.28), channel_id=1, source_target_pairs={{0,4},{2,6},{4,2},{6,0},{1,5},{3,7},{5,3},{7,1},{8,12},{10,14},{12... | collective-permute-start | bytes 98312 | tf_op jit(solution)/shard_map/cond/branch_0_fun/ppermute | solution.py:313
  14.6 4.8 %collective-permute-start.1 = (bf16[128,128]{1,0:T(8,128)(2,1)S(1)}, bf16[128,128]{1,0:T(8,128)(2,1)S(1)}, u32[]{:S(2)}, u32[]{:S(2)}) collective-permute-start(bf16[128,128]{1,0:T(8,128)(2,1)S(1)} %get-tuple-element.29), channel_id=1, source_target_pairs={{0,6},{2,4},{4,0},{6,2},{1,7},{3,5},{5,1},{7,3},{8,14},{10,12},{12... | collective-permute-start | bytes 98312 | tf_op jit(solution)/shard_map/cond/branch_0_fun/ppermute | solution.py:313
  15.6 4.1 %collective-permute-start.2 = (bf16[128,128]{1,0:T(8,128)(2,1)S(1)}, bf16[128,128]{1,0:T(8,128)(2,1)S(1)}, u32[]{:S(2)}, u32[]{:S(2)}) collective-permute-start(bf16[128,128]{1,0:T(8,128)(2,1)S(1)} %get-tuple-element.30), channel_id=1, source_target_pairs={{0,2},{2,0},{4,6},{6,4},{1,3},{3,1},{5,7},{7,5},{8,10},{10,8},{12,... | collective-permute-start | bytes 98312 | tf_op jit(solution)/shard_map/cond/branch_0_fun/ppermute | solution.py:313
